TPU v7x, 512 devices: a whole 4x4x16 slice. The times are simulated.
512 devices in a mesh: dp: 64 (over z_lo, y, core), fsdp: 8 (over x, z_hi).
Axes of the slice: x: 4, y: 4, z: 16 (z_hi: 2, z_lo: 8; z = z_hi * 8 + z_lo), core: 2. Of those that a mesh axis runs over, the one named last changes fastest.
Arguments:
- tokens: bfloat16 [512, 16384], P('dp', 'fsdp'), may hold values from -6 to 6
- route_plan: int32 [4], replicated, may hold values from -1 to 3, as said below
- block_tokens: int32 [4], replicated, may hold values from 1 to 128
- gate_up: bfloat16 [16384, 2, 26624], P('fsdp', None, 'dp'), may hold values from -0.046875 to 0.046875
- down_proj: bfloat16 [26624, 16384], P('dp', 'fsdp'), may hold values from -0.0390625 to 0.0390625
Outputs:
- layer_output: bfloat16 [512, 16384], P('dp', 'fsdp')
Inputs may be any that keep to these rules, and one draw needn't show every extreme that they name: route_plan[b] is -1 for an empty source block; no two source blocks name the same destination block.
All inputs are finite; a program needn't handle non-finite values.
Results may differ from a plain program's by a relative error of at most 0.0049.
Values may be sent and summed in bfloat16 or wider, within the bound.
No kernel may reach another device: no remote copies, remote signals or barrier semaphores. Data moves between devices by JAX's collectives and lax.ppermute only.
A program may use at most 64 MiB of HBM per device.

v0:
```python
import jax
import jax.numpy as jnp
from jax import lax
from jax.sharding import PartitionSpec as P

BLK = 128


def activate(summed, hidden_width):
    return (jax.nn.silu(summed[:, :hidden_width]) * summed[:, hidden_width:]).astype(jnp.bfloat16)


def live_only(piece, block_tokens):
    block_count = block_tokens.shape[0]
    row_ids = lax.broadcasted_iota(jnp.int32, (piece.shape[0], 1), 0)
    block_of = row_ids // BLK
    limits = jnp.sum(
        jnp.where(
            block_of == jnp.arange(block_count, dtype=jnp.int32)[None, :], block_tokens[None, :], 0
        ),
        axis=1,
        keepdims=True,
    )
    return jnp.where(row_ids % BLK < limits, piece, jnp.zeros_like(piece))


def body(tokens, route_plan, block_tokens, gate_up, down_proj):
    feature_part = gate_up.shape[0]
    hidden_part = gate_up.shape[2]
    weights = gate_up.reshape(feature_part, 2 * hidden_part)
    block_count = block_tokens.shape[0]
    partial_sum = jnp.dot(
        live_only(lax.all_gather(tokens, "dp", axis=0, tiled=True), block_tokens),
        weights,
        preferred_element_type=jnp.float32,
    )
    hidden = activate(lax.psum(partial_sum, "fsdp"), hidden_part)
    row_total = hidden.shape[0]
    select = (route_plan[None, :] == jnp.arange(block_count, dtype=jnp.int32)[:, None]).astype(
        jnp.bfloat16
    )
    delivered = jnp.dot(
        select, hidden.reshape(block_count, -1), preferred_element_type=jnp.float32
    ).astype(jnp.bfloat16)
    delivered = delivered.reshape(row_total, hidden_part)
    summed_out = lax.psum_scatter(
        jnp.dot(delivered, down_proj, preferred_element_type=jnp.float32),
        "dp",
        scatter_dimension=0,
        tiled=True,
    )
    return summed_out.astype(jnp.bfloat16)


def solution(mesh):
    return jax.shard_map(
        body,
        mesh=mesh,
        in_specs=(P("dp", "fsdp"), P(), P(), P("fsdp", None, "dp"), P("dp", "fsdp")),
        out_specs=P("dp", "fsdp"),
        check_vma=False,
    )
```

profile of v0, /device:TPU:2, one launch (start us, length us, event | category | flops | bytes accessed | tf_op | source)
XLA Modules:
  0.0 920.6 jit_solution(6259264659617768471)
XLA Ops:
  6.5 0.0 copy-start
  6.5 0.0 all-gather.2.cloned.1.call-start
  6.5 0.7 all-gather.2.cloned.1.call-update
  7.3 0.0 all-reduce.2.cloned.1.call-start
  7.3 1.0 select_reduce_fusion
  8.3 126.4 %all-gather.2.cloned.1.call-done = bf16[512,2048]{1,0:T(8,128)(2,1)} async-done(((bf16[8,2048]{1,0:T(8,128)(2,1)}), bf16[512,2048]{1,0:T(8,128)(2,1)}) %all-gather.2.cloned.1.call-update) | async-done | bytes 2097168 | tf_op jit(solution)/shard_map/all_gather | solution.py:33
  134.7 0.0 copy-done
  134.7 4.8 fusion
  139.5 0.0 all-reduce.2.cloned.1.call-update
  139.6 0.0 copy-start.1
  139.6 0.0 reduce-scatter.2.cloned.1.call-start
  139.6 311.9 %all-reduce.2.cloned.1.call-done = f32[512,832]{0,1:T(8,128)} async-done(((f32[512,832]{0,1:T(8,128)}), f32[512,832]{0,1:T(8,128)}) %all-reduce.2.cloned.1.call-update) | async-done | bytes 1703952 | tf_op jit(solution)/shard_map/psum | solution.py:37
  451.5 2.4 fusion.4
  454.0 2.0 copy.7
  456.0 2.6 reshape.68
  458.5 0.0 copy-done.1
  458.5 2.1 convolution_convert_fusion
  460.7 2.6 reshape.69
  463.3 4.8 fusion.13
  468.1 0.0 reduce-scatter.2.cloned.1.call-update
  468.1 444.5 %reduce-scatter.2.cloned.1.call-done = f32[8,2048]{1,0:T(8,128)} async-done(((f32[512,2048]{1,0:T(8,128)}), f32[8,2048]{1,0:T(8,128)}) %reduce-scatter.2.cloned.1.call-update) | async-done | bytes 65552 | tf_op jit(solution)/shard_map/reduce_scatter | solution.py:46
  912.7 1.5 convert_element_type.12
  (2 shorter events, 0.0 us)
Async XLA Ops:
  6.5 128.2 %copy-start = (bf16[2048,2,416]{0,2,1:T(8,128)(2,1)S(1)}, bf16[2048,2,416]{0,2,1:T(8,128)(2,1)}, u32[]{:S(2)}) copy-start(bf16[2048,2,416]{0,2,1:T(8,128)(2,1)} %param.8) | copy-start | bytes 10223620
  6.5 128.2 %all-gather.2.cloned.1.call-start = ((), (), s32[]{:S(2)}) async-start(), calls=%async_computation.1 | async-start | bytes 2129920 | tf_op jit(solution)/shard_map/all_gather | solution.py:33
  7.3 444.3 %all-reduce.2.cloned.1.call-start = ((), (), s32[]{:S(2)}) async-start(), calls=%async_computation.2 | async-start | bytes 3407872 | tf_op jit(solution)/shard_map/psum | solution.py:37
  139.6 319.0 %copy-start.1 = (s32[4]{0:T(128)S(1)}, s32[4]{0:T(128)}, u32[]{:S(2)}) copy-start(s32[4]{0:T(128)} %param.6) | copy-start | bytes 52
  139.6 773.1 %reduce-scatter.2.cloned.1.call-start = ((), (), s32[]{:S(2)}) async-start(), calls=%async_computation.3 | async-start | bytes 4259840 | tf_op jit(solution)/shard_map/reduce_scatter | solution.py:46
Sparse Core Ops, SparseCore 0:
  9.5 125.1 all-gather.1
  139.7 311.8 all-reduce.1
  468.3 444.3 reduce-scatter.1
where the time goes:
time: 921 us
  waiting for transfers between devices  884 us (96%)
  between operations  13.1 us (1%)
  matrix products  11.8 us (1%)
    reduce_scatter x1, waiting for transfers between devices, body(): lax.psum_scatter(jnp.dot(delivered, down_proj, preferred_element_type=jnp...  445 us
    psum x1, waiting for transfers between devices, body(): hidden = activate(lax.psum(partial_sum, 'fsdp'), hidden_part)  312 us
    all_gather x1, waiting for transfers between devices, body(): lax.all_gather(tokens, 'dp', axis=0, tiled=True)  126 us
  transfers between devices with their start and end apart: 3, of which 3 were waited for; matrix products, arithmetic and copies ran while one was open for 0% of the time, Pallas kernels for 0%

commit v1 on v0

v1 whole, which is shorter than its diff:
```python
import functools

import jax
import jax.numpy as jnp
from jax import lax
from jax.experimental import pallas as pl
from jax.experimental.pallas import tpu as pltpu
from jax.sharding import Mesh
from jax.sharding import PartitionSpec as P

BLK = 128
HALF = 64
ZL, YY, CC, XX, ZH = 8, 4, 2, 4, 2
SIZES = (8,)
BF16, F32 = jnp.bfloat16, jnp.float32


def halves_of(plan, lives):
    slot = jnp.int32(0)
    for h in range(ZL):
        block, part = h // 2, h % 2
        live = (plan(block) >= 0) & (lives(block) > HALF * part)
        yield h, block, part, live, slot
        slot = slot + live.astype(jnp.int32)


def pack_kernel(slots, plan_ref, lives_ref, place_ref, rows_ref, out_ref):
    row = lax.broadcasted_iota(jnp.int32, rows_ref.shape[1:], 0) + place_ref[0]
    count = jnp.int32(0)
    for h, block, part, live, slot in halves_of(lambda b: plan_ref[b], lambda b: lives_ref[b]):
        count = slot + live.astype(jnp.int32)

        @pl.when(live)
        def _():
            kept = row + HALF * part < lives_ref[block]
            rows = jnp.where(kept, rows_ref[h].astype(F32), 0.0).astype(BF16)
            for copy in range(YY):
                out_ref[copy, slot] = rows

    for s in range(slots):

        @pl.when(s >= count)
        def _():
            for copy in range(YY):
                out_ref[copy, s] = jnp.zeros(out_ref.shape[2:], BF16)


def place_kernel(plan_ref, lives_ref, parts_ref, out_ref):
    out_ref[...] = jnp.zeros(out_ref.shape, BF16)
    for h, block, part, live, slot in halves_of(lambda b: plan_ref[b], lambda b: lives_ref[b]):

        @pl.when(live)
        def _():
            total = parts_ref[0, slot].astype(F32)
            for k in range(1, YY):
                total = total + parts_ref[k, slot].astype(F32)
            out_ref[2 * plan_ref[block] + part] = total.astype(BF16)


def local_call(kernel, scalars, shape):
    return pl.pallas_call(
        kernel,
        out_shape=jax.ShapeDtypeStruct(shape, BF16),
        in_specs=[pl.BlockSpec(memory_space=pltpu.SMEM)] * scalars + [pl.BlockSpec(memory_space=pltpu.VMEM)],
        out_specs=pl.BlockSpec(memory_space=pltpu.VMEM),
        compiler_params=pltpu.CompilerParams(vmem_limit_bytes=16 << 20),
    )


def exchange(array, axis):
    return lax.all_to_all(array, axis, 0, 0, tiled=False)


def swap(array, axis):
    return lax.ppermute(array, axis, [(0, 1), (1, 0)])


def spread(array, copies):
    return jnp.broadcast_to(array[None], (copies,) + array.shape)


def block_rows(slots, gathered, plan, lives, weights, down):
    features, hidden = weights.shape[0], down.shape[0]
    per = slots * 8
    place = (lax.axis_index("y") * 16 + lax.axis_index("c") * 8).reshape(1)
    packed = local_call(functools.partial(pack_kernel, slots), 3, (YY, slots, 8, features))(plan, lives, place, gathered)
    mine = exchange(packed.reshape(YY, per, features), "y").reshape(YY * per, features)
    rows = jnp.concatenate([mine, swap(mine, "c")], axis=0)
    total = rows.shape[0]

    share = hidden // XX
    partial = lax.dot_general(
        weights.transpose(1, 2, 0).reshape(2 * hidden, features), rows, (((1,), (1,)), ((), ())), preferred_element_type=F32
    )
    partial = partial.reshape(2, XX, share, total).transpose(1, 0, 2, 3)
    along_x = jnp.sum(exchange(partial, "x"), axis=0)
    other = swap(along_x.astype(BF16), "zh").astype(F32)
    summed = along_x + other
    act = (jax.nn.silu(summed[0]) * summed[1]).astype(BF16)
    act = exchange(spread(act, XX), "x").reshape(hidden, total)

    def project(part):
        return lax.dot_general(part, down, (((0,), (0,)), ((), ())), preferred_element_type=F32)

    theirs = swap(project(act[:, total // 2 :]), "c")
    ours = (project(act[:, : total // 2]) + theirs).astype(BF16)
    parts = exchange(ours.reshape(YY, per, -1), "y").reshape(YY, slots, 8, -1)
    return local_call(place_kernel, 2, (ZL, 8, down.shape[1]))(plan, lives, parts)


def body(tokens, plan, lives, weights, down):
    gathered = exchange(spread(tokens, ZL), "zl")
    if len(SIZES) == 1:
        placed = block_rows(SIZES[0], gathered, plan, lives, weights, down)
    else:
        count = jnp.sum((plan >= 0) * (1 + (lives > HALF)))
        which = sum((count > n).astype(jnp.int32) for n in SIZES[:-1])
        placed = lax.switch(
            which, [functools.partial(block_rows, n) for n in SIZES], gathered, plan, lives, weights, down
        )
    sums = exchange(placed, "zl")
    total = sums[0].astype(F32)
    for k in range(1, ZL):
        total = total + sums[k].astype(F32)
    return total.astype(BF16)


def solution(mesh):
    fine = Mesh(mesh.devices.reshape(ZL, YY, CC, XX, ZH), ("zl", "y", "c", "x", "zh"))
    dp, fsdp = ("zl", "y", "c"), ("x", "zh")
    return jax.shard_map(
        body,
        mesh=fine,
        in_specs=(P(dp, fsdp), P(), P(), P(fsdp, None, dp), P(dp, fsdp)),
        out_specs=P(dp, fsdp),
        check_vma=False,
    )
```

time: 921 us -> 180 us (0.20)
  the two profiles are of different devices: /device:TPU:2 before, /device:TPU:32 now
where the time goes in v1:
time: 180 us; the launch traced here: 179 us
  blocking collectives  100 us (56%)
  waiting for transfers between devices  40.7 us (23%)
  starting transfers between devices  24.7 us (14%)
  other arithmetic  5.38 us (3%)
  matrix products  3.41 us (2%)
  local copies, waits for them, and re-layouts  3.15 us (2%)
    all_to_all x5, blocking collectives, exchange(): return lax.all_to_all(array, axis, 0, 0, tiled=False)  100 us
    ppermute x3, waiting for transfers between devices, swap(): return lax.ppermute(array, axis, [(0, 1), (1, 0)])  24.4 us
    all_to_all x1, waiting for transfers between devices, exchange(): return lax.all_to_all(array, axis, 0, 0, tiled=False)  16.4 us
    all_to_all x1, starting transfers between devices, exchange(): return lax.all_to_all(array, axis, 0, 0, tiled=False)  12.6 us
    ppermute x3, starting transfers between devices, swap(): return lax.ppermute(array, axis, [(0, 1), (1, 0)])  12 us
  transfers between devices with their start and end apart: 4, of which 4 were waited for; matrix products, arithmetic and copies ran while one was open for 0% of the time, Pallas kernels for 0%

profile of v1, /device:TPU:32, one launch (start us, length us, event | category | flops | bytes accessed | tf_op | source)
XLA Modules:
  0.0 179.3 jit_solution(6061708076816002672)
XLA Ops:
  0.0 1.6 broadcast_in_dim.6
  1.6 12.6 %all-to-all-start = ((bf16[8,8,2048]{2,1,0:T(8,128)(2,1)}), bf16[8,8,2048]{2,1,0:T(8,128)(2,1)}, u32[]{:S(2)}, u32[]{:S(2)}) async-start(bf16[8,8,2048]{2,1,0:T(8,128)(2,1)} %broadcast_in_dim.6), calls=%async_computation | async-start | bytes 524288 | tf_op jit(solution)/shard_map/all_to_all | solution.py:71
  14.3 16.4 %all-to-all-done.rows_ref = bf16[8,8,2048]{2,1,0:T(8,128)(2,1)} async-done(((bf16[8,8,2048]{2,1,0:T(8,128)(2,1)}), bf16[8,8,2048]{2,1,0:T(8,128)(2,1)}, u32[]{:S(2)}, u32[]{:S(2)}) %all-to-all-start) | async-done | bytes 262176 | tf_op jit(solution)/shard_map/all_to_all | solution.py:71
  30.7 0.7 copy-done.1
  32.0 1.1 shard_map.55
  33.1 15.2 %all_to_all.30 = bf16[4,64,2048]{2,1,0:T(8,128)(2,1)S(1)} all-to-all(bf16[4,64,2048]{2,1,0:T(8,128)(2,1)S(1)} %bitcast.23), channel_id=1, replica_groups=mesh['zl'=8,'y'=4,'c'=2,'x'=4,'zh'=2] {'y'}, dimensions={0} | all-to-all | bytes 2097152 | tf_op jit(solution)/shard_map/all_to_all | solution.py:71
  48.3 1.9 %collective-permute-start = (bf16[256,2048]{1,0:T(8,128)(2,1)S(1)}, bf16[256,2048]{1,0:T(8,128)(2,1)S(1)}, u32[]{:S(2)}, u32[]{:S(2)}) collective-permute-start(bf16[256,2048]{1,0:T(8,128)(2,1)S(1)} %bitcast.30), channel_id=1, source_target_pairs={{0,8},{8,0},{1,9},{9,1},{2,10},{10,2},{3,11},{11,3},{4,12},{12,4},... | collective-permute-start | bytes 3145736 | tf_op jit(solution)/shard_map/ppermute | solution.py:75
  50.2 2.6 %collective-permute-done = bf16[256,2048]{1,0:T(8,128)(2,1)S(1)} collective-permute-done((bf16[256,2048]{1,0:T(8,128)(2,1)S(1)}, bf16[256,2048]{1,0:T(8,128)(2,1)S(1)}, u32[]{:S(2)}, u32[]{:S(2)}) %collective-permute-start) | collective-permute-done | bytes 1048608 | tf_op jit(solution)/shard_map/ppermute | solution.py:75
  52.8 2.0 %fusion.1 = f32[512,832]{0,1:T(8,128)S(1)} fusion(bf16[832,2048]{1,0:T(8,128)(2,1)S(1)} %bitcast.22, bf16[256,2048]{1,0:T(8,128)(2,1)S(1)} %collective-permute-done, bf16[256,2048]{1,0:T(8,128)(2,1)S(1)} %bitcast.31), kind=kOutput, calls=%fused_computation.2 | convolution fusion | flops 1749024768 | bytes 7208960 | tf_op jit(solution)/shard_map/dot_general | solution.py:92
  54.9 26.6 %all_to_all.31 = f32[4,2,104,512]{3,2,1,0:T(8,128)} all-to-all(f32[4,2,104,512]{3,2,1,0:T(8,128)S(1)} %bitcast.25), channel_id=1, replica_groups=mesh['zl'=8,'y'=4,'c'=2,'x'=4,'zh'=2] {'x'}, dimensions={0} | all-to-all | bytes 3407872 | tf_op jit(solution)/shard_map/all_to_all | solution.py:71
  81.6 2.4 %reduce_sum.9 = f32[2,104,512]{2,1,0:T(8,128)} reduce(f32[4,2,104,512]{3,2,1,0:T(8,128)} %all_to_all.31, f32[]{:T(128)} %constant.18.clone.1), dimensions={0}, to_apply=%region_0.0 | reduce | flops 319488 | bytes 2129924 | tf_op jit(solution)/shard_map/reduce_sum | solution.py:96
  84.0 1.2 convert_element_type.56
  85.2 8.2 %collective-permute-start.1 = (bf16[2,104,512]{2,1,0:T(8,128)(2,1)S(1)}, bf16[2,104,512]{2,1,0:T(8,128)(2,1)S(1)}, u32[]{:S(2)}, u32[]{:S(2)}) collective-permute-start(bf16[2,104,512]{2,1,0:T(8,128)(2,1)S(1)} %convert_element_type.56), channel_id=1, source_target_pairs={{0,1},{1,0},{2,3},{3,2},{4,5},{5,4},{6,7},{7,6},{8,9},{9,8},{10,11... | collective-permute-start | bytes 638984 | tf_op jit(solution)/shard_map/ppermute | solution.py:75
  93.4 17.6 %collective-permute-done.1 = bf16[2,104,512]{2,1,0:T(8,128)(2,1)S(1)} collective-permute-done((bf16[2,104,512]{2,1,0:T(8,128)(2,1)S(1)}, bf16[2,104,512]{2,1,0:T(8,128)(2,1)S(1)}, u32[]{:S(2)}, u32[]{:S(2)}) %collective-permute-start.1) | collective-permute-done | bytes 213024 | tf_op jit(solution)/shard_map/ppermute | solution.py:75
  111.0 1.1 convert_add_fusion
  112.2 10.1 %all_to_all.32 = bf16[4,104,512]{2,1,0:T(8,128)(2,1)S(1)} all-to-all(bf16[4,104,512]{2,1,0:T(8,128)(2,1)S(1)} %broadcast_in_dim.16), channel_id=1, replica_groups=mesh['zl'=8,'y'=4,'c'=2,'x'=4,'zh'=2] {'x'}, dimensions={0} | all-to-all | bytes 851968 | tf_op jit(solution)/shard_map/all_to_all | solution.py:71
  122.3 0.7 fusion.5
  123.0 1.9 %collective-permute-start.2 = (f32[256,2048]{1,0:T(8,128)S(1)}, f32[256,2048]{1,0:T(8,128)S(1)}, u32[]{:S(2)}, u32[]{:S(2)}) collective-permute-start(f32[256,2048]{1,0:T(8,128)S(1)} %fusion.5), channel_id=1, source_target_pairs={{0,8},{8,0},{1,9},{9,1},{2,10},{10,2},{3,11},{11,3},{4,12},{12,4},... | collective-permute-start | bytes 6291464 | tf_op jit(solution)/shard_map/ppermute | solution.py:75
  124.9 4.1 %collective-permute-done.2 = f32[256,2048]{1,0:T(8,128)S(1)} collective-permute-done((f32[256,2048]{1,0:T(8,128)S(1)}, f32[256,2048]{1,0:T(8,128)S(1)}, u32[]{:S(2)}, u32[]{:S(2)}) %collective-permute-start.2) | collective-permute-done | bytes 2097184 | tf_op jit(solution)/shard_map/ppermute | solution.py:75
  129.1 0.7 fusion
  129.8 18.1 %all_to_all.33 = bf16[4,64,2048]{2,1,0:T(8,128)(2,1)S(1)} all-to-all(bf16[4,64,2048]{2,1,0:T(8,128)(2,1)S(1)} %bitcast.26), channel_id=1, replica_groups=mesh['zl'=8,'y'=4,'c'=2,'x'=4,'zh'=2] {'y'}, dimensions={0} | all-to-all | bytes 2097152 | tf_op jit(solution)/shard_map/all_to_all | solution.py:71
  147.9 0.7 shard_map.56
  148.6 30.0 %all_to_all.34 = bf16[8,8,2048]{2,1,0:T(8,128)(2,1)S(1)} all-to-all(bf16[8,8,2048]{2,1,0:T(8,128)(2,1)S(1)} %shard_map.56), channel_id=1, replica_groups=mesh['zl'=8,'y'=4,'c'=2,'x'=4,'zh'=2] {'zl'}, dimensions={0} | all-to-all | bytes 524288 | tf_op jit(solution)/shard_map/all_to_all | solution.py:71
  178.6 0.7 fusion.10
  (14 shorter events, 0.9 us)
Async XLA Ops:
  0.0 52.8 %copy-start = (bf16[2048,2,416]{0,2,1:T(8,128)(2,1)S(1)}, bf16[2048,2,416]{0,2,1:T(8,128)(2,1)}, u32[]{:S(2)}) copy-start(bf16[2048,2,416]{0,2,1:T(8,128)(2,1)} %param.8) | copy-start | bytes 10223620
  1.6 29.0 %all-to-all-start = ((bf16[8,8,2048]{2,1,0:T(8,128)(2,1)}), bf16[8,8,2048]{2,1,0:T(8,128)(2,1)}, u32[]{:S(2)}, u32[]{:S(2)}) async-start(bf16[8,8,2048]{2,1,0:T(8,128)(2,1)} %broadcast_in_dim.6), calls=%async_computation | async-start | bytes 524288 | tf_op jit(solution)/shard_map/all_to_all | solution.py:71
  30.7 0.7 copy-start.1
  31.3 0.7 copy-start.3
  48.3 4.5 %collective-permute-start = (bf16[256,2048]{1,0:T(8,128)(2,1)S(1)}, bf16[256,2048]{1,0:T(8,128)(2,1)S(1)}, u32[]{:S(2)}, u32[]{:S(2)}) collective-permute-start(bf16[256,2048]{1,0:T(8,128)(2,1)S(1)} %bitcast.30), channel_id=1, source_target_pairs={{0,8},{8,0},{1,9},{9,1},{2,10},{10,2},{3,11},{11,3},{4,12},{12,4},... | collective-permute-start | bytes 3145736 | tf_op jit(solution)/shard_map/ppermute | solution.py:75
  84.0 38.3 %copy-start.5 = (bf16[416,2048]{1,0:T(8,128)(2,1)S(1)}, bf16[416,2048]{1,0:T(8,128)(2,1)}, u32[]{:S(2)}) copy-start(bf16[416,2048]{1,0:T(8,128)(2,1)} %param.9) | copy-start | bytes 5111812
  85.2 25.8 %collective-permute-start.1 = (bf16[2,104,512]{2,1,0:T(8,128)(2,1)S(1)}, bf16[2,104,512]{2,1,0:T(8,128)(2,1)S(1)}, u32[]{:S(2)}, u32[]{:S(2)}) collective-permute-start(bf16[2,104,512]{2,1,0:T(8,128)(2,1)S(1)} %convert_element_type.56), channel_id=1, source_target_pairs={{0,1},{1,0},{2,3},{3,2},{4,5},{5,4},{6,7},{7,6},{8,9},{9,8},{10,11... | collective-permute-start | bytes 638984 | tf_op jit(solution)/shard_map/ppermute | solution.py:75
  123.0 6.1 %collective-permute-start.2 = (f32[256,2048]{1,0:T(8,128)S(1)}, f32[256,2048]{1,0:T(8,128)S(1)}, u32[]{:S(2)}, u32[]{:S(2)}) collective-permute-start(f32[256,2048]{1,0:T(8,128)S(1)} %fusion.5), channel_id=1, source_target_pairs={{0,8},{8,0},{1,9},{9,1},{2,10},{10,2},{3,11},{11,3},{4,12},{12,4},... | collective-permute-start | bytes 6291464 | tf_op jit(solution)/shard_map/ppermute | solution.py:75
  129.8 18.1 %copy-start.2 = (s32[4]{0:T(128)S(1)}, s32[4]{0:T(128)}, u32[]{:S(2)}) copy-start(s32[4]{0:T(128)} %plan_ref.3) | copy-start | bytes 52
  129.8 18.1 %copy-start.4 = (s32[4]{0:T(128)S(1)}, s32[4]{0:T(128)}, u32[]{:S(2)}) copy-start(s32[4]{0:T(128)} %lives_ref.3) | copy-start | bytes 52

commit v2 on v1

--- a/solution.py
+++ b/solution.py
@@ -11,7 +11,7 @@
 BLK = 128
 HALF = 64
 ZL, YY, CC, XX, ZH = 8, 4, 2, 4, 2
-SIZES = (8,)
+SIZES = (2, 4, 6, 8)
 BF16, F32 = jnp.bfloat16, jnp.float32
 
 

time: 180 us -> 141 us (0.78)
  blocking collectives: 100 us -> 75.4 us
  waiting for transfers between devices: 40.7 us -> 28.7 us
  other arithmetic: 5.38 us -> 2.1 us
  between operations: 0.12 us -> 1.96 us
    all_to_all x5, blocking collectives: 100 us -> 75.4 us  [exchange(): return lax.all_to_all(array, axis, 0, 0, tiled=False)]
    ppermute x3, waiting for transfers between devices: 24.4 us -> 15.7 us  [swap(): return lax.ppermute(array, axis, [(0, 1), (1, 0)])]
    all_to_all x1, waiting for transfers between devices: 16.4 us -> 13 us  [exchange(): return lax.all_to_all(array, axis, 0, 0, tiled=False)]
    reduce_sum x1, other arithmetic: 2.43 us -> 0.05 us  [block_rows(): along_x = jnp.sum(exchange(partial, 'x'), axis=0)]
  transfers between devices with their start and end apart: 4 -> 4, of which waited for: 4 -> 4; matrix products, arithmetic and copies ran while one was open for 0% -> 1% of each run, Pallas kernels for 0% -> 0%
where the time goes in v2:
time: 141 us; the launch traced here: 140 us
  blocking collectives  75.4 us (53%)
  waiting for transfers between devices  28.7 us (20%)
  starting transfers between devices  24.8 us (18%)
  matrix products  4.04 us (3%)
  other arithmetic  2.1 us (1%)
  between operations  1.96 us (1%)
  local copies, waits for them, and re-layouts  1.58 us (1%)
  Pallas kernels  1.47 us (1%)
    all_to_all x5, blocking collectives, exchange(): return lax.all_to_all(array, axis, 0, 0, tiled=False)  75.4 us
    ppermute x3, waiting for transfers between devices, swap(): return lax.ppermute(array, axis, [(0, 1), (1, 0)])  15.7 us
    all_to_all x1, waiting for transfers between devices, exchange(): return lax.all_to_all(array, axis, 0, 0, tiled=False)  13 us
    all_to_all x1, starting transfers between devices, exchange(): return lax.all_to_all(array, axis, 0, 0, tiled=False)  12.6 us
    ppermute x3, starting transfers between devices, swap(): return lax.ppermute(array, axis, [(0, 1), (1, 0)])  12.2 us
    dot_general x1, matrix products, block_rows(): lax.dot_general(weights.transpose(1, 2, 0).reshape(2 * hidden, features),...  3.1 us
  transfers between devices with their start and end apart: 4, of which 4 were waited for; matrix products, arithmetic and copies ran while one was open for 1% of the time, Pallas kernels for 0%

profile of v2, /device:TPU:32, one launch (start us, length us, event | category | flops | bytes accessed | tf_op | source)
XLA Modules:
  0.0 140.5 jit_solution(319928031198762785)
XLA Ops:
  0.0 1.5 %broadcast_in_dim.30 = bf16[8,8,2048]{2,1,0:T(8,128)(2,1)} broadcast(bf16[8,2048]{1,0:T(8,128)(2,1)} %param.9), dimensions={1,2} | broadcast | bytes 294912 | tf_op jit(solution)/shard_map/broadcast_in_dim | solution.py:79
  1.5 12.6 %all-to-all-start.16 = ((bf16[8,8,2048]{2,1,0:T(8,128)(2,1)}), bf16[8,8,2048]{2,1,0:T(8,128)(2,1)S(1)}, u32[]{:S(2)}, u32[]{:S(2)}) async-start(bf16[8,8,2048]{2,1,0:T(8,128)(2,1)} %broadcast_in_dim.30), calls=%async_computation.16 | async-start | bytes 524288 | tf_op jit(solution)/shard_map/all_to_all | solution.py:71
  14.1 1.3 fusion.45
  17.4 13.0 %all-to-all-done.16 = bf16[8,8,2048]{2,1,0:T(8,128)(2,1)S(1)} async-done(((bf16[8,8,2048]{2,1,0:T(8,128)(2,1)}), bf16[8,8,2048]{2,1,0:T(8,128)(2,1)S(1)}, u32[]{:S(2)}, u32[]{:S(2)}) %all-to-all-start.16) | async-done | bytes 262176 | tf_op jit(solution)/shard_map/all_to_all | solution.py:71
  30.4 85.1 %conditional.1 = (bf16[8,8,2048]{2,1,0:T(8,128)(2,1)S(1)}) conditional(s32[]{:T(128)} %clamp.3, (s32[4]{0:T(128)}, s32[4]{0:T(128)}, bf16[8,8,2048]{2,1,0:T(8,128)(2,1)S(1)}, bf16[2048,2,416]{0,2,1:T(8,128)(2,1)}, bf16[416,2048]{1,0:T(8,128)(2,1)}) %tuple.17, (s32[4]{0:T(128)}, s32[4]{0:T(128)}, ...), branch_computations={%region_1.3_spmd, %region_3.5_spmd, %region_5.7_spmd, %region_7.9_... | conditional | flops 2623447040 | bytes 66929112 | solution.py:118
  30.4 0.8 branch_1_fun.2
  31.2 12.3 %all_to_all.78 = bf16[4,32,2048]{2,1,0:T(8,128)(2,1)S(1)} all-to-all(bf16[4,32,2048]{2,1,0:T(8,128)(2,1)S(1)} %bitcast.86), channel_id=1, replica_groups=mesh['zl'=8,'y'=4,'c'=2,'x'=4,'zh'=2] {'y'}, dimensions={0} | all-to-all | bytes 1048576 | tf_op jit(solution)/shard_map/cond/branch_1_fun/all_to_all | solution.py:71
  43.5 1.9 %collective-permute-start.3 = (bf16[128,2048]{1,0:T(8,128)(2,1)S(1)}, bf16[128,2048]{1,0:T(8,128)(2,1)S(1)}, u32[]{:S(2)}, u32[]{:S(2)}) collective-permute-start(bf16[128,2048]{1,0:T(8,128)(2,1)S(1)} %bitcast.120), channel_id=1, source_target_pairs={{0,8},{8,0},{1,9},{9,1},{2,10},{10,2},{3,11},{11,3},{4,12},{12,4},... | collective-permute-start | bytes 1572872 | tf_op jit(solution)/shard_map/cond/branch_1_fun/ppermute | solution.py:75
  45.5 1.9 %collective-permute-done.3 = bf16[128,2048]{1,0:T(8,128)(2,1)S(1)} collective-permute-done((bf16[128,2048]{1,0:T(8,128)(2,1)S(1)}, bf16[128,2048]{1,0:T(8,128)(2,1)S(1)}, u32[]{:S(2)}, u32[]{:S(2)}) %collective-permute-start.3) | collective-permute-done | bytes 524320 | tf_op jit(solution)/shard_map/cond/branch_1_fun/ppermute | solution.py:75
  47.3 3.1 %fusion.12 = f32[256,832]{0,1:T(8,128)S(1)} fusion(bf16[832,2048]{1,0:T(8,128)(2,1)} %bitcast.94, bf16[128,2048]{1,0:T(8,128)(2,1)S(1)} %collective-permute-done.3, bf16[128,2048]{1,0:T(8,128)(2,1)S(1)} %bitcast.121), kind=kOutput, calls=%fused_computation.17 | convolution fusion | flops 874512384 | bytes 5308416 | tf_op jit(solution)/shard_map/cond/branch_1_fun/dot_general | solution.py:92
  50.4 0.1 copy.19
  50.5 17.4 %all_to_all.79 = f32[4,2,104,256]{3,2,1,0:T(8,128)S(1)} all-to-all(f32[4,2,104,256]{3,2,1,0:T(8,128)S(1)} %bitcast.97), channel_id=1, replica_groups=mesh['zl'=8,'y'=4,'c'=2,'x'=4,'zh'=2] {'x'}, dimensions={0} | all-to-all | bytes 1703936 | tf_op jit(solution)/shard_map/cond/branch_1_fun/all_to_all | solution.py:71
  67.9 0.1 reduce_sum.41
  68.0 8.4 %collective-permute-start.4 = (bf16[2,104,256]{2,1,0:T(8,128)(2,1)S(1)}, bf16[2,104,256]{2,1,0:T(8,128)(2,1)S(1)}, u32[]{:S(2)}, u32[]{:S(2)}) collective-permute-start(bf16[2,104,256]{2,1,0:T(8,128)(2,1)S(1)} %convert_element_type.79), channel_id=1, source_target_pairs={{0,1},{1,0},{2,3},{3,2},{4,5},{5,4},{6,7},{7,6},{8,9},{9,8},{10,11... | collective-permute-start | bytes 319496 | tf_op jit(solution)/shard_map/cond/branch_1_fun/ppermute | solution.py:75
  76.3 11.2 %collective-permute-done.4 = bf16[2,104,256]{2,1,0:T(8,128)(2,1)S(1)} collective-permute-done((bf16[2,104,256]{2,1,0:T(8,128)(2,1)S(1)}, bf16[2,104,256]{2,1,0:T(8,128)(2,1)S(1)}, u32[]{:S(2)}, u32[]{:S(2)}) %collective-permute-start.4) | collective-permute-done | bytes 106528 | tf_op jit(solution)/shard_map/cond/branch_1_fun/ppermute | solution.py:75
  87.7 8.9 %all_to_all.80 = bf16[4,104,256]{2,1,0:T(8,128)(2,1)S(1)} all-to-all(bf16[4,104,256]{2,1,0:T(8,128)(2,1)S(1)} %broadcast_in_dim.20), channel_id=1, replica_groups=mesh['zl'=8,'y'=4,'c'=2,'x'=4,'zh'=2] {'x'}, dimensions={0} | all-to-all | bytes 425984 | tf_op jit(solution)/shard_map/cond/branch_1_fun/all_to_all | solution.py:71
  96.6 0.5 fusion.16
  97.1 1.9 %collective-permute-start.5 = (f32[128,2048]{1,0:T(8,128)S(1)}, f32[128,2048]{1,0:T(8,128)S(1)}, u32[]{:S(2)}, u32[]{:S(2)}) collective-permute-start(f32[128,2048]{1,0:T(8,128)S(1)} %fusion.16), channel_id=1, source_target_pairs={{0,8},{8,0},{1,9},{9,1},{2,10},{10,2},{3,11},{11,3},{4,12},{12,4},... | collective-permute-start | bytes 3145736 | tf_op jit(solution)/shard_map/cond/branch_1_fun/ppermute | solution.py:75
  99.0 2.6 %collective-permute-done.5 = f32[128,2048]{1,0:T(8,128)S(1)} collective-permute-done((f32[128,2048]{1,0:T(8,128)S(1)}, f32[128,2048]{1,0:T(8,128)S(1)}, u32[]{:S(2)}, u32[]{:S(2)}) %collective-permute-start.5) | collective-permute-done | bytes 1048608 | tf_op jit(solution)/shard_map/cond/branch_1_fun/ppermute | solution.py:75
  101.7 0.5 fusion.11
  102.1 12.5 %all_to_all.81 = bf16[4,32,2048]{2,1,0:T(8,128)(2,1)S(1)} all-to-all(bf16[4,32,2048]{2,1,0:T(8,128)(2,1)S(1)} %bitcast.99), channel_id=1, replica_groups=mesh['zl'=8,'y'=4,'c'=2,'x'=4,'zh'=2] {'y'}, dimensions={0} | all-to-all | bytes 1048576 | tf_op jit(solution)/shard_map/cond/branch_1_fun/all_to_all | solution.py:71
  114.6 0.7 branch_1_fun.3
  115.5 24.3 %all_to_all.90 = bf16[8,8,2048]{2,1,0:T(8,128)(2,1)S(1)} all-to-all(bf16[8,8,2048]{2,1,0:T(8,128)(2,1)S(1)} %get-tuple-element.90), channel_id=1, replica_groups=mesh['zl'=8,'y'=4,'c'=2,'x'=4,'zh'=2] {'zl'}, dimensions={0} | all-to-all | bytes 524288 | tf_op jit(solution)/shard_map/all_to_all | solution.py:71
  139.8 0.7 fusion.44
  (10 shorter events, 0.1 us)
Async XLA Ops:
  1.5 28.9 %all-to-all-start.16 = ((bf16[8,8,2048]{2,1,0:T(8,128)(2,1)}), bf16[8,8,2048]{2,1,0:T(8,128)(2,1)S(1)}, u32[]{:S(2)}, u32[]{:S(2)}) async-start(bf16[8,8,2048]{2,1,0:T(8,128)(2,1)} %broadcast_in_dim.30), calls=%async_computation.16 | async-start | bytes 524288 | tf_op jit(solution)/shard_map/all_to_all | solution.py:71
  43.5 3.8 %collective-permute-start.3 = (bf16[128,2048]{1,0:T(8,128)(2,1)S(1)}, bf16[128,2048]{1,0:T(8,128)(2,1)S(1)}, u32[]{:S(2)}, u32[]{:S(2)}) collective-permute-start(bf16[128,2048]{1,0:T(8,128)(2,1)S(1)} %bitcast.120), channel_id=1, source_target_pairs={{0,8},{8,0},{1,9},{9,1},{2,10},{10,2},{3,11},{11,3},{4,12},{12,4},... | collective-permute-start | bytes 1572872 | tf_op jit(solution)/shard_map/cond/branch_1_fun/ppermute | solution.py:75
  67.9 28.7 %copy-start.1 = (bf16[416,2048]{1,0:T(8,128)(2,1)S(1)}, bf16[416,2048]{1,0:T(8,128)(2,1)}, u32[]{:S(2)}) copy-start(bf16[416,2048]{1,0:T(8,128)(2,1)} %get-tuple-element.59) | copy-start | bytes 5111812 | tf_op jit(solution)/shard_map/cond
  68.0 19.6 %collective-permute-start.4 = (bf16[2,104,256]{2,1,0:T(8,128)(2,1)S(1)}, bf16[2,104,256]{2,1,0:T(8,128)(2,1)S(1)}, u32[]{:S(2)}, u32[]{:S(2)}) collective-permute-start(bf16[2,104,256]{2,1,0:T(8,128)(2,1)S(1)} %convert_element_type.79), channel_id=1, source_target_pairs={{0,1},{1,0},{2,3},{3,2},{4,5},{5,4},{6,7},{7,6},{8,9},{9,8},{10,11... | collective-permute-start | bytes 319496 | tf_op jit(solution)/shard_map/cond/branch_1_fun/ppermute | solution.py:75
  97.1 17.5 %copy-start.6 = (s32[4]{0:T(128)S(1)}, s32[4]{0:T(128)}, u32[]{:S(2)}) copy-start(s32[4]{0:T(128)} %get-tuple-element.55.plan_ref) | copy-start | bytes 52 | tf_op jit(solution)/shard_map/cond
  97.1 17.5 %copy-start.10 = (s32[4]{0:T(128)S(1)}, s32[4]{0:T(128)}, u32[]{:S(2)}) copy-start(s32[4]{0:T(128)} %get-tuple-element.56.lives_ref) | copy-start | bytes 52 | tf_op jit(solution)/shard_map/cond
  97.1 4.6 %collective-permute-start.5 = (f32[128,2048]{1,0:T(8,128)S(1)}, f32[128,2048]{1,0:T(8,128)S(1)}, u32[]{:S(2)}, u32[]{:S(2)}) collective-permute-start(f32[128,2048]{1,0:T(8,128)S(1)} %fusion.16), channel_id=1, source_target_pairs={{0,8},{8,0},{1,9},{9,1},{2,10},{10,2},{3,11},{11,3},{4,12},{12,4},... | collective-permute-start | bytes 3145736 | tf_op jit(solution)/shard_map/cond/branch_1_fun/ppermute | solution.py:75

commit v3 on v2

--- a/solution.py
+++ b/solution.py
@@ -11,7 +11,7 @@
 BLK = 128
 HALF = 64
 ZL, YY, CC, XX, ZH = 8, 4, 2, 4, 2
-SIZES = (2, 4, 6, 8)
+SIZES = (2, 3, 4, 5, 6, 8)
 BF16, F32 = jnp.bfloat16, jnp.float32
 
 
@@ -80,36 +80,31 @@
 
 
 def block_rows(slots, gathered, plan, lives, weights, down):
-    features, hidden = weights.shape[0], down.shape[0]
+    features, hidden = weights.shape[2], down.shape[0]
     per = slots * 8
     place = (lax.axis_index("y") * 16 + lax.axis_index("c") * 8).reshape(1)
     packed = local_call(functools.partial(pack_kernel, slots), 3, (YY, slots, 8, features))(plan, lives, place, gathered)
-    mine = exchange(packed.reshape(YY, per, features), "y").reshape(YY * per, features)
-    rows = jnp.concatenate([mine, swap(mine, "c")], axis=0)
-    total = rows.shape[0]
+    rows = exchange(packed.reshape(YY, per, features), "y").reshape(YY * per, features)
 
-    share = hidden // XX
     partial = lax.dot_general(
-        weights.transpose(1, 2, 0).reshape(2 * hidden, features), rows, (((1,), (1,)), ((), ())), preferred_element_type=F32
+        rows, weights.reshape(2 * hidden, features), (((1,), (1,)), ((), ())), preferred_element_type=F32
     )
-    partial = partial.reshape(2, XX, share, total).transpose(1, 0, 2, 3)
-    along_x = jnp.sum(exchange(partial, "x"), axis=0)
+    along_x = jnp.sum(exchange(partial.reshape(XX, per, 2 * hidden), "x"), axis=0)
     other = swap(along_x.astype(BF16), "zh").astype(F32)
     summed = along_x + other
-    act = (jax.nn.silu(summed[0]) * summed[1]).astype(BF16)
-    act = exchange(spread(act, XX), "x").reshape(hidden, total)
+    act = (jax.nn.silu(summed[:, :hidden]) * summed[:, hidden:]).astype(BF16)
+    act = exchange(spread(act, XX), "x").reshape(XX * per, hidden)
 
-    def project(part):
-        return lax.dot_general(part, down, (((0,), (0,)), ((), ())), preferred_element_type=F32)
-
-    theirs = swap(project(act[:, total // 2 :]), "c")
-    ours = (project(act[:, : total // 2]) + theirs).astype(BF16)
+    ours = jnp.dot(act, down, preferred_element_type=F32).astype(BF16)
     parts = exchange(ours.reshape(YY, per, -1), "y").reshape(YY, slots, 8, -1)
     return local_call(place_kernel, 2, (ZL, 8, down.shape[1]))(plan, lives, parts)
 
 
 def body(tokens, plan, lives, weights, down):
     gathered = exchange(spread(tokens, ZL), "zl")
+    weights = weights.transpose(1, 2, 0)
+    weights = jnp.concatenate([weights, swap(weights, "c")], axis=1)
+    down = jnp.concatenate([down, swap(down, "c")], axis=0)
     if len(SIZES) == 1:
         placed = block_rows(SIZES[0], gathered, plan, lives, weights, down)
     else:

time: 141 us -> 133 us (0.943)
  waiting for transfers between devices: 28.7 us -> 14.6 us
  other arithmetic: 2.1 us -> 14.2 us
  blocking collectives: 75.4 us -> 64.7 us
  matrix products: 4.04 us -> 5.96 us
    all_to_all x5, blocking collectives: 75.4 us -> 64.7 us  [exchange(): return lax.all_to_all(array, axis, 0, 0, tiled=False)]
    all_to_all x1, waiting for transfers between devices: 13 us -> 3.15 us  [exchange(): return lax.all_to_all(array, axis, 0, 0, tiled=False)]
    concatenate x0 -> x2, other arithmetic: none -> 8.39 us  [the longest x1 5.82 us: body(): weights = jnp.concatenate([weights, swap(weights, 'c')], axis=1)]
    ppermute x3, waiting for transfers between devices: 15.7 us -> 11.5 us  [swap(): return lax.ppermute(array, axis, [(0, 1), (1, 0)])]
    dot_general x3 -> x2, matrix products: 4.04 us -> 5.96 us  [the longest x1 5.24 us: block_rows(): lax.dot_general(rows, weights.reshape(2 * hidden, features), (((1,), (1,)...]
    reduce_sum x1, other arithmetic: 0.05 us -> 1.89 us  [block_rows(): jnp.sum(exchange(partial.reshape(XX, per, 2 * hidden), 'x'), axis=0)]
  transfers between devices with their start and end apart: 4 -> 4, of which waited for: 4 -> 2; matrix products, arithmetic and copies ran while one was open for 1% -> 8% of each run, Pallas kernels for 0% -> 0%
where the time goes in v3:
time: 133 us; the launch traced here: 132 us
  blocking collectives  64.7 us (49%)
  starting transfers between devices  25.2 us (19%)
  waiting for transfers between devices  14.6 us (11%)
  other arithmetic  14.2 us (11%)
  matrix products  5.96 us (4%)
  between operations  3.32 us (2%)
  Pallas kernels  2.5 us (2%)
  local copies, waits for them, and re-layouts  1.89 us (1%)
    all_to_all x5, blocking collectives, exchange(): return lax.all_to_all(array, axis, 0, 0, tiled=False)  64.7 us
    all_to_all x1, starting transfers between devices, exchange(): return lax.all_to_all(array, axis, 0, 0, tiled=False)  12.6 us
    ppermute x3, starting transfers between devices, swap(): return lax.ppermute(array, axis, [(0, 1), (1, 0)])  12.5 us
    ppermute x3, waiting for transfers between devices, swap(): return lax.ppermute(array, axis, [(0, 1), (1, 0)])  11.5 us
    concatenate x1, other arithmetic, body(): weights = jnp.concatenate([weights, swap(weights, 'c')], axis=1)  5.82 us
    dot_general x1, matrix products, block_rows(): lax.dot_general(rows, weights.reshape(2 * hidden, features), (((1,), (1,)...  5.24 us
    all_to_all x1, waiting for transfers between devices, exchange(): return lax.all_to_all(array, axis, 0, 0, tiled=False)  3.15 us
  transfers between devices with their start and end apart: 4, of which 2 were waited for; matrix products, arithmetic and copies ran while one was open for 8% of the time, Pallas kernels for 0%

profile of v3, /device:TPU:32, one launch (start us, length us, event | category | flops | bytes accessed | tf_op | source)
XLA Modules:
  0.0 132.5 jit_solution(491065084353961286)
XLA Ops:
  0.0 1.9 %collective-permute-start.6 = (bf16[2,416,2048]{2,1,0:T(8,128)(2,1)}, bf16[2,416,2048]{2,1,0:T(8,128)(2,1)}, u32[]{:S(2)}, u32[]{:S(2)}) collective-permute-start(bf16[2,416,2048]{2,1,0:T(8,128)(2,1)} %bitcast.93), channel_id=1, source_target_pairs={{0,8},{8,0},{1,9},{9,1},{2,10},{10,2},{3,11},{11,3},{4,12},{12,4},... | collective-permute-start | bytes 10223624 | tf_op jit(solution)/shard_map/ppermute | solution.py:75
  1.9 2.4 %collective-permute-start.7 = (bf16[416,2048]{1,0:T(8,128)(2,1)}, bf16[416,2048]{1,0:T(8,128)(2,1)}, u32[]{:S(2)}, u32[]{:S(2)}) collective-permute-start(bf16[416,2048]{1,0:T(8,128)(2,1)} %param.15), channel_id=1, source_target_pairs={{0,8},{8,0},{1,9},{9,1},{2,10},{10,2},{3,11},{11,3},{4,12},{12,4},... | collective-permute-start | bytes 5111816 | tf_op jit(solution)/shard_map/ppermute | solution.py:75
  4.3 1.5 %broadcast_in_dim.22 = bf16[8,8,2048]{2,1,0:T(8,128)(2,1)} broadcast(bf16[8,2048]{1,0:T(8,128)(2,1)} %param.11), dimensions={1,2} | broadcast | bytes 294912 | tf_op jit(solution)/shard_map/broadcast_in_dim | solution.py:79
  5.8 12.6 %all-to-all-start.24 = ((bf16[8,8,2048]{2,1,0:T(8,128)(2,1)}), bf16[8,8,2048]{2,1,0:T(8,128)(2,1)}, u32[]{:S(2)}, u32[]{:S(2)}) async-start(bf16[8,8,2048]{2,1,0:T(8,128)(2,1)} %broadcast_in_dim.22), calls=%async_computation.24 | async-start | bytes 524288 | tf_op jit(solution)/shard_map/all_to_all | solution.py:71
  18.5 1.3 fusion.7
  23.0 2.6 %pad_maximum_fusion.1 = bf16[832,2048]{1,0:T(8,128)(2,1)S(1)} fusion(bf16[416,2048]{1,0:T(8,128)(2,1)} %collective-permute-done.7, bf16[416,2048]{1,0:T(8,128)(2,1)} %param.15), kind=kLoop, calls=%fused_computation.25 | loop fusion | flops 6815744 | bytes 6815744 | tf_op jit(solution)/shard_map/concatenate | solution.py:107
  26.0 5.8 %pad_maximum_fusion = bf16[2,832,2048]{2,1,0:T(8,128)(2,1)} fusion(bf16[2,416,2048]{2,1,0:T(8,128)(2,1)} %collective-permute-done.6, bf16[2,416,2048]{2,1,0:T(8,128)(2,1)S(1)} %bitcast.94), kind=kLoop, calls=%fused_computation.24 | loop fusion | flops 13631488 | bytes 13631488 | tf_op jit(solution)/shard_map/concatenate | solution.py:106
  31.8 3.2 %all-to-all-done.24 = bf16[8,8,2048]{2,1,0:T(8,128)(2,1)} async-done(((bf16[8,8,2048]{2,1,0:T(8,128)(2,1)}), bf16[8,8,2048]{2,1,0:T(8,128)(2,1)}, u32[]{:S(2)}, u32[]{:S(2)}) %all-to-all-start.24) | async-done | bytes 262176 | tf_op jit(solution)/shard_map/all_to_all | solution.py:71
  35.0 77.8 %conditional.1 = (bf16[8,8,2048]{2,1,0:T(8,128)(2,1)}) conditional(s32[]{:T(128)} %clamp.3, (s32[4]{0:T(128)S(1)}, s32[4]{0:T(128)S(1)}, bf16[8,8,2048]{2,1,0:T(8,128)(2,1)}, bf16[2,832,2048]{2,1,0:T(8,128)(2,1)}, bf16[832,2048]{1,0:T(8,128)(2,1)S(1)}) %tuple.36, (s32[4]{0:T(128)S(1)}, s32[4]{0:T(128)S(1)}, ...), branch_computations={%region_1.3_spmd, %region_3.5_spmd, %region_5.7_spmd, %region_7.9_... | conditional | flops 2618728448 | bytes 28655768 | solution.py:113
  35.0 1.1 branch_2_fun.2
  36.1 12.3 %all_to_all.114 = bf16[4,32,2048]{2,1,0:T(8,128)(2,1)S(1)} all-to-all(bf16[4,32,2048]{2,1,0:T(8,128)(2,1)S(1)} %bitcast.81), channel_id=1, replica_groups=mesh['zl'=8,'y'=4,'c'=2,'x'=4,'zh'=2] {'y'}, dimensions={0} | all-to-all | bytes 1048576 | tf_op jit(solution)/shard_map/cond/branch_2_fun/all_to_all | solution.py:71
  48.4 5.2 %fusion.11 = f32[4,32,1664]{2,1,0:T(8,128)S(1)} fusion(bf16[4,32,2048]{2,1,0:T(8,128)(2,1)S(1)} %all_to_all.114, bf16[1664,2048,1]{1,0,2:T(8,128)(2,1)} %bitcast.89), kind=kOutput, calls=%fused_computation.34 | convolution fusion | flops 872415232 | bytes 8192000 | tf_op jit(solution)/shard_map/cond/branch_2_fun/dot_general | solution.py:89
  53.7 14.0 %all_to_all.115 = f32[4,32,1664]{2,1,0:T(8,128)} all-to-all(f32[4,32,1664]{2,1,0:T(8,128)S(1)} %fusion.11), channel_id=1, replica_groups=mesh['zl'=8,'y'=4,'c'=2,'x'=4,'zh'=2] {'x'}, dimensions={0} | all-to-all | bytes 1703936 | tf_op jit(solution)/shard_map/cond/branch_2_fun/all_to_all | solution.py:71
  67.7 1.9 %reduce_sum.58 = f32[32,1664]{1,0:T(8,128)} reduce(f32[4,32,1664]{2,1,0:T(8,128)} %all_to_all.115, f32[]{:T(128)} %constant.90.clone), dimensions={0}, to_apply=%region_6.6 | reduce | flops 159744 | bytes 1064964 | tf_op jit(solution)/shard_map/cond/branch_2_fun/reduce_sum | solution.py:92
  69.6 0.9 convert_element_type.99
  70.6 8.2 %collective-permute-start.2 = (bf16[32,1664]{1,0:T(8,128)(2,1)S(1)}, bf16[32,1664]{1,0:T(8,128)(2,1)S(1)}, u32[]{:S(2)}, u32[]{:S(2)}) collective-permute-start(bf16[32,1664]{1,0:T(8,128)(2,1)S(1)} %convert_element_type.99), channel_id=1, source_target_pairs={{0,1},{1,0},{2,3},{3,2},{4,5},{5,4},{6,7},{7,6},{8,9},{9,8},{10,11... | collective-permute-start | bytes 319496 | tf_op jit(solution)/shard_map/cond/branch_2_fun/ppermute | solution.py:75
  78.8 11.5 %collective-permute-done.2 = bf16[32,1664]{1,0:T(8,128)(2,1)S(1)} collective-permute-done((bf16[32,1664]{1,0:T(8,128)(2,1)S(1)}, bf16[32,1664]{1,0:T(8,128)(2,1)S(1)}, u32[]{:S(2)}, u32[]{:S(2)}) %collective-permute-start.2) | collective-permute-done | bytes 106528 | tf_op jit(solution)/shard_map/cond/branch_2_fun/ppermute | solution.py:75
  90.2 1.0 convert_add_fusion.2
  91.3 8.9 %all_to_all.116 = bf16[4,32,832]{2,1,0:T(8,128)(2,1)S(1)} all-to-all(bf16[4,32,832]{2,1,0:T(8,128)(2,1)S(1)} %broadcast_in_dim.7), channel_id=1, replica_groups=mesh['zl'=8,'y'=4,'c'=2,'x'=4,'zh'=2] {'x'}, dimensions={0} | all-to-all | bytes 425984 | tf_op jit(solution)/shard_map/cond/branch_2_fun/all_to_all | solution.py:71
  100.2 0.7 convolution_convert_fusion.2
  100.9 10.5 %all_to_all.117 = bf16[4,32,2048]{2,1,0:T(8,128)(2,1)S(1)} all-to-all(bf16[4,32,2048]{2,1,0:T(8,128)(2,1)S(1)} %bitcast.97), channel_id=1, replica_groups=mesh['zl'=8,'y'=4,'c'=2,'x'=4,'zh'=2] {'y'}, dimensions={0} | all-to-all | bytes 1048576 | tf_op jit(solution)/shard_map/cond/branch_2_fun/all_to_all | solution.py:71
  111.4 1.4 %branch_2_fun.3 = bf16[8,8,2048]{2,1,0:T(8,128)(2,1)} custom-call(s32[4]{0:T(128)S(1)} %get-tuple-element.82.plan_ref, s32[4]{0:T(128)S(1)} %get-tuple-element.83.lives_ref, bf16[4,4,8,2048]{3,2,1,0:T(8,128)(2,1)S(1)} %bitcast.82), custom_call_target="tpu_custom_call" | custom-call | tf_op jit(solution)/shard_map/cond/branch_2_fun/pallas_call | solution.py:100
  112.8 19.0 %all_to_all.130 = bf16[8,8,2048]{2,1,0:T(8,128)(2,1)S(1)} all-to-all(bf16[8,8,2048]{2,1,0:T(8,128)(2,1)} %get-tuple-element.102), channel_id=1, replica_groups=mesh['zl'=8,'y'=4,'c'=2,'x'=4,'zh'=2] {'zl'}, dimensions={0} | all-to-all | bytes 524288 | tf_op jit(solution)/shard_map/all_to_all | solution.py:71
  131.8 0.7 fusion.6
  (10 shorter events, 0.5 us)
Async XLA Ops:
  0.0 25.6 %collective-permute-start.6 = (bf16[2,416,2048]{2,1,0:T(8,128)(2,1)}, bf16[2,416,2048]{2,1,0:T(8,128)(2,1)}, u32[]{:S(2)}, u32[]{:S(2)}) collective-permute-start(bf16[2,416,2048]{2,1,0:T(8,128)(2,1)} %bitcast.93), channel_id=1, source_target_pairs={{0,8},{8,0},{1,9},{9,1},{2,10},{10,2},{3,11},{11,3},{4,12},{12,4},... | collective-permute-start | bytes 10223624 | tf_op jit(solution)/shard_map/ppermute | solution.py:75
  1.9 21.1 %collective-permute-start.7 = (bf16[416,2048]{1,0:T(8,128)(2,1)}, bf16[416,2048]{1,0:T(8,128)(2,1)}, u32[]{:S(2)}, u32[]{:S(2)}) collective-permute-start(bf16[416,2048]{1,0:T(8,128)(2,1)} %param.15), channel_id=1, source_target_pairs={{0,8},{8,0},{1,9},{9,1},{2,10},{10,2},{3,11},{11,3},{4,12},{12,4},... | collective-permute-start | bytes 5111816 | tf_op jit(solution)/shard_map/ppermute | solution.py:75
  5.8 29.2 %all-to-all-start.24 = ((bf16[8,8,2048]{2,1,0:T(8,128)(2,1)}), bf16[8,8,2048]{2,1,0:T(8,128)(2,1)}, u32[]{:S(2)}, u32[]{:S(2)}) async-start(bf16[8,8,2048]{2,1,0:T(8,128)(2,1)} %broadcast_in_dim.22), calls=%async_computation.24 | async-start | bytes 524288 | tf_op jit(solution)/shard_map/all_to_all | solution.py:71
  23.0 3.0 %copy-start = (bf16[2048,2,416]{0,2,1:T(8,128)(2,1)S(1)}, bf16[2048,2,416]{0,2,1:T(8,128)(2,1)}, u32[]{:S(2)}) copy-start(bf16[2048,2,416]{0,2,1:T(8,128)(2,1)} %param.14) | copy-start | bytes 10223620
  25.6 9.4 %copy-start.1 = (s32[4]{0:T(128)S(1)}, s32[4]{0:T(128)}, u32[]{:S(2)}) copy-start(s32[4]{0:T(128)} %param.12) | copy-start | bytes 52
  25.6 9.4 %copy-start.2 = (s32[4]{0:T(128)S(1)}, s32[4]{0:T(128)}, u32[]{:S(2)}) copy-start(s32[4]{0:T(128)} %param.13) | copy-start | bytes 52
  70.6 19.7 %collective-permute-start.2 = (bf16[32,1664]{1,0:T(8,128)(2,1)S(1)}, bf16[32,1664]{1,0:T(8,128)(2,1)S(1)}, u32[]{:S(2)}, u32[]{:S(2)}) collective-permute-start(bf16[32,1664]{1,0:T(8,128)(2,1)S(1)} %convert_element_type.99), channel_id=1, source_target_pairs={{0,1},{1,0},{2,3},{3,2},{4,5},{5,4},{6,7},{7,6},{8,9},{9,8},{10,11... | collective-permute-start | bytes 319496 | tf_op jit(solution)/shard_map/cond/branch_2_fun/ppermute | solution.py:75
